TPU v7x, 32 devices: a whole 2x2x4 slice. The times are simulated.
32 devices in a mesh: groups: 2 (over y), space: 8 (over z, x), dp: 2 (over core).
Axes of the slice: x: 2, y: 2, z: 4, core: 2. Of those that a mesh axis runs over, the one named last changes fastest.
Arguments:
- tokens: bfloat16 [8, 16, 64, 768], P('groups', 'dp', 'space'), parts along dimension 0, may hold values from -45 to 45
- cotangent: bfloat16 [8, 16, 64, 768], P('groups', 'dp', 'space'), parts along dimension 0, may hold values from -6 to 6
- region: int32 [8, 16, 64], P('groups', 'dp', 'space'), parts along dimension 0, may hold values from 0 to 3
- qkv_weight: bfloat16 [768, 2304], P(('space', 'dp')), may hold values from -0.21875 to 0.21875
- proj_weight: bfloat16 [768, 768], P(None, ('space', 'dp')), may hold values from -0.21875 to 0.21875
- logit_scale: float32 [12], replicated, may hold values from 2 to 25
Outputs:
- block_output: bfloat16 [8, 16, 64, 768], P('groups', 'dp', 'space'), parts along dimension 0
- token_grad: bfloat16 [8, 16, 64, 768], P('groups', 'dp', 'space'), parts along dimension 0
- proj_grad: float32 [1536, 768], P('groups', ('space', 'dp')), parts along dimension 0
There are 2 independent parts, one for each index of `groups`. A program takes and returns all parts, laid end to end along the dimension named above; an argument that names none is the same for every part. Nothing has to cross between parts.
Inputs may be any that keep to these rules, and one draw needn't show every extreme that they name: region[d, h, w] labels the token that sits at position (d, h, w) of the shifted grid, that is tokens[(d + 2) mod 4, (h + 4) mod 16, (w + 4) mod 64].
All inputs are finite; a program needn't handle non-finite values.
Results may differ from a plain program's by a relative error of at most 0.012.
The roundings to bfloat16 on the way count: a program that leaves them out, or rounds other values in their place, can miss the bound.
Values may be sent and summed in bfloat16 or wider, within the bound.
A program may use at most 64 MiB of HBM per device.

v0:
```python
import math

import jax
import jax.numpy as jnp
from jax import lax
from jax.sharding import PartitionSpec as P

HEAD_GROUP = 4
WD = 4
WH = 8
WW = 8
SD = 2
SH = 4
SW = 4


def shifted_2(value, axis, steps):
    count = lax.axis_size(axis)
    pairs = [(source, (source + steps) % count) for source in range(count)]
    return lax.ppermute(value, axis, pairs)


def to_windows(field):
    depth_cells, height_cells, width_cells = (field.shape[0], field.shape[1], field.shape[2])
    trailing = tuple(field.shape[3:])
    blocked = field.reshape(
        (depth_cells // WD, WD, height_cells // WH, WH, width_cells // WW, WW) + trailing
    )
    axes_order = (0, 2, 4, 1, 3, 5) + tuple(range(6, 6 + len(trailing)))
    return blocked.transpose(axes_order).reshape((-1, WD * WH * WW) + trailing)


def from_windows(windowed, depth_cells, height_cells, width_cells):
    trailing = tuple(windowed.shape[2:])
    blocked = windowed.reshape(
        (depth_cells // WD, height_cells // WH, width_cells // WW, WD, WH, WW) + trailing
    )
    axes_order = (0, 3, 1, 4, 2, 5) + tuple(range(6, 6 + len(trailing)))
    return blocked.transpose(axes_order).reshape(
        (depth_cells, height_cells, width_cells) + trailing
    )


def product(pattern, left_side, right_side):
    return jnp.einsum(pattern, left_side, right_side, preferred_element_type=jnp.float32)


def head_forward(piece_qkv, allowed, scales):
    queries = piece_qkv[:, :, :, 0].astype(jnp.float32)
    key_rows = piece_qkv[:, :, :, 1].astype(jnp.float32)
    values = piece_qkv[:, :, :, 2]
    query_inv = lax.rsqrt(jnp.sum(queries * queries, axis=-1, keepdims=True) + 1e-06)
    key_inv = lax.rsqrt(jnp.sum(key_rows * key_rows, axis=-1, keepdims=True) + 1e-06)
    query_unit = queries * query_inv
    key_unit = key_rows * key_inv
    query_low = query_unit.astype(jnp.bfloat16)
    key_low = key_unit.astype(jnp.bfloat16)
    scores = product("wqhd,wkhd->whqk", query_low, key_low) * scales[None, :, None, None]
    raised = jnp.where(allowed[:, None], jnp.exp(scores), 0.0)
    probability = raised / jnp.sum(raised, axis=-1, keepdims=True)
    prob_low = probability.astype(jnp.bfloat16)
    return (
        query_unit,
        key_unit,
        query_inv,
        key_inv,
        query_low,
        key_low,
        values,
        probability,
        prob_low,
    )


def window_block(windows_x, windows_g, windows_region, qkv_full, proj_full, logit_scale):
    window_count, window_size, channels = windows_x.shape
    head_count = logit_scale.shape[0]
    inner_width = proj_full.shape[0]
    head_size = inner_width // head_count
    group_count = head_count // HEAD_GROUP
    flat_rows = windows_x.reshape(window_count * window_size, channels)
    packed = jnp.dot(flat_rows, qkv_full, preferred_element_type=jnp.float32).astype(jnp.bfloat16)
    packed = packed.reshape(window_count, window_size, head_count, 3, head_size)
    allowed = windows_region[:, :, None] == windows_region[:, None, :]
    group_ids = jnp.arange(group_count, dtype=jnp.int32)

    def group_pieces(group_index):
        piece_qkv = lax.dynamic_slice_in_dim(packed, group_index * HEAD_GROUP, HEAD_GROUP, 2)
        scales = lax.dynamic_slice_in_dim(logit_scale, group_index * HEAD_GROUP, HEAD_GROUP, 0)
        return (piece_qkv, scales)

    def forward_group(group_index):
        piece_qkv, scales = group_pieces(group_index)
        outs_fwd = head_forward(piece_qkv, allowed, scales)
        return product("whqk,wkhd->wqhd", outs_fwd[8], outs_fwd[6]).astype(jnp.bfloat16)

    attended = lax.map(forward_group, group_ids)
    attended = jnp.moveaxis(attended, 0, 2).reshape(window_count * window_size, inner_width)
    mixed_rows = jnp.dot(attended, proj_full, preferred_element_type=jnp.float32)
    centered = mixed_rows - jnp.mean(mixed_rows, axis=-1, keepdims=True)
    inv_dev = lax.rsqrt(jnp.mean(centered * centered, axis=-1, keepdims=True) + 1e-05)
    normed = centered * inv_dev
    branch = normed.astype(jnp.bfloat16)
    grad_in = windows_g.reshape(window_count * window_size, channels).astype(jnp.float32)
    grad_mixed = inv_dev * (
        grad_in
        - jnp.mean(grad_in, axis=-1, keepdims=True)
        - normed * jnp.mean(grad_in * normed, axis=-1, keepdims=True)
    )
    grad_low = grad_mixed.astype(jnp.bfloat16)
    proj_term = lax.dot_general(
        attended, grad_low, (((0,), (0,)), ((), ())), preferred_element_type=jnp.float32
    )
    grad_att = lax.dot_general(
        grad_low, proj_full, (((1,), (1,)), ((), ())), preferred_element_type=jnp.float32
    )
    grad_att = grad_att.astype(jnp.bfloat16).reshape(
        window_count, window_size, head_count, head_size
    )

    def backward_group(group_index):
        piece_qkv, scales = group_pieces(group_index)
        (
            query_unit,
            key_unit,
            query_inv,
            key_inv,
            query_low,
            key_low,
            values,
            probability,
            prob_low,
        ) = head_forward(piece_qkv, allowed, scales)
        grad_piece = lax.dynamic_slice_in_dim(grad_att, group_index * HEAD_GROUP, HEAD_GROUP, 2)
        grad_prob = product("wqhd,wkhd->whqk", grad_piece, values)
        grad_values = product("whqk,wqhd->wkhd", prob_low, grad_piece)
        grad_scores = probability * (
            grad_prob - jnp.sum(probability * grad_prob, axis=-1, keepdims=True)
        )
        scaled_low = (grad_scores * scales[None, :, None, None]).astype(jnp.bfloat16)
        grad_qunit = product("whqk,wkhd->wqhd", scaled_low, key_low)
        grad_kunit = product("whqk,wqhd->wkhd", scaled_low, query_low)
        grad_query = query_inv * (
            grad_qunit - query_unit * jnp.sum(grad_qunit * query_unit, axis=-1, keepdims=True)
        )
        grad_key = key_inv * (
            grad_kunit - key_unit * jnp.sum(grad_kunit * key_unit, axis=-1, keepdims=True)
        )
        return jnp.stack([grad_query, grad_key, grad_values], axis=3).astype(jnp.bfloat16)

    grad_packed = lax.map(backward_group, group_ids)
    grad_packed = jnp.moveaxis(grad_packed, 0, 2).reshape(
        window_count * window_size, 3 * inner_width
    )
    grad_rows = lax.dot_general(
        grad_packed, qkv_full, (((1,), (1,)), ((), ())), preferred_element_type=jnp.float32
    )
    grad_rows = grad_rows.astype(jnp.bfloat16)
    return (
        branch.reshape(window_count, window_size, channels),
        grad_rows.reshape(window_count, window_size, channels),
        proj_term,
    )


def shards(tokens, cotangent, region, qkv_weight, proj_weight, logit_scale):
    depth_cells, height_cells, width_cells, channels = tokens.shape
    rim_pair = jnp.stack([tokens[:, :, :SW], cotangent[:, :, :SW]])
    arrived = shifted_2(rim_pair, "space", -1)
    across_tok = jnp.concatenate([tokens[:, :, SW:], arrived[0]], axis=2)
    across_grad = jnp.concatenate([cotangent[:, :, SW:], arrived[1]], axis=2)
    row_pair = jnp.stack([across_tok[:, :SH], across_grad[:, :SH]])
    arrived_rows = shifted_2(row_pair, "dp", -1)
    shifted = jnp.roll(jnp.concatenate([across_tok[:, SH:], arrived_rows[0]], axis=1), -SD, axis=0)
    shifted_grad = jnp.roll(
        jnp.concatenate([across_grad[:, SH:], arrived_rows[1]], axis=1), -SD, axis=0
    )
    qkv_full, proj_full = (
        lax.all_gather(qkv_weight, ("space", "dp"), axis=0, tiled=True),
        lax.all_gather(proj_weight, ("space", "dp"), axis=1, tiled=True),
    )
    branch_w, grad_w, proj_term = window_block(
        to_windows(shifted),
        to_windows(shifted_grad),
        to_windows(region),
        qkv_full,
        proj_full,
        logit_scale,
    )
    branch = jnp.roll(from_windows(branch_w, depth_cells, height_cells, width_cells), SD, axis=0)
    grad_grid = jnp.roll(from_windows(grad_w, depth_cells, height_cells, width_cells), SD, axis=0)
    back_rows = jnp.stack([branch[:, -SH:], grad_grid[:, -SH:]])
    came_rows = shifted_2(back_rows, "dp", 1)
    branch = jnp.concatenate([came_rows[0], branch[:, :-SH]], axis=1)
    grad_grid = jnp.concatenate([came_rows[1], grad_grid[:, :-SH]], axis=1)
    back_rims = jnp.stack([branch[:, :, -SW:], grad_grid[:, :, -SW:]])
    came_rims = shifted_2(back_rims, "space", 1)
    branch = jnp.concatenate([came_rims[0], branch[:, :, :-SW]], axis=2)
    grad_grid = jnp.concatenate([came_rims[1], grad_grid[:, :, :-SW]], axis=2)
    block_output = (tokens.astype(jnp.float32) + branch.astype(jnp.float32)).astype(jnp.bfloat16)
    token_grad = (cotangent.astype(jnp.float32) + grad_grid.astype(jnp.float32)).astype(
        jnp.bfloat16
    )
    summed = lax.psum_scatter(proj_term, ("space", "dp"), scatter_dimension=1, tiled=True)
    token_total = (
        depth_cells * height_cells * width_cells * lax.axis_size("space") * lax.axis_size("dp")
    )
    proj_grad = summed * (1.0 / math.sqrt(token_total))
    return (block_output, token_grad, proj_grad)


def solution(mesh):
    in_specs = (
        P("groups", "dp", "space", None),
        P("groups", "dp", "space", None),
        P("groups", "dp", "space"),
        P(("space", "dp"), None),
        P(None, ("space", "dp")),
        P(),
    )
    out_specs = (
        P("groups", "dp", "space", None),
        P("groups", "dp", "space", None),
        P("groups", ("space", "dp")),
    )
    return jax.shard_map(shards, mesh=mesh, in_specs=in_specs, out_specs=out_specs, check_vma=False)
```

profile of v0, /device:TPU:0, one launch (start us, length us, event | category | flops | bytes accessed | tf_op | source)
XLA Modules:
  0.0 177.3 jit_solution(17538478673784831901)
XLA Ops:
  7.9 1.7 slice_bitcast_fusion.10
  10.0 6.0 %collective-permute-start = (bf16[2,4,8,4,768]{4,3,2,1,0:T(4,128)(2,1)S(1)}, bf16[2,4,8,4,768]{4,3,2,1,0:T(4,128)(2,1)S(1)}, u32[]{:S(2)}, u32[]{:S(2)}) collective-permute-start(bf16[2,4,8,4,768]{4,3,2,1,0:T(4,128)(2,1)S(1)} %pad_maximum_fusion.5), channel_id=1, source_target_pairs={{0,14},{2,0},{4,2},{6,4},{8,6},{10,8},{12,10},{14,12},{1,15},{3,1}... | collective-permute-start | bytes 1179656 | tf_op jit(solution)/shard_map/ppermute | solution.py:20
  16.0 12.0 %collective-permute-done = bf16[2,4,8,4,768]{4,3,2,1,0:T(4,128)(2,1)S(1)} collective-permute-done((bf16[2,4,8,4,768]{4,3,2,1,0:T(4,128)(2,1)S(1)}, bf16[2,4,8,4,768]{4,3,2,1,0:T(4,128)(2,1)S(1)}, u32[]{:S(2)}, u32[]{:S(2)}) %collective-permute-start) | collective-permute-done | bytes 393248 | tf_op jit(solution)/shard_map/ppermute | solution.py:20
  29.0 1.4 collective-permute-done.1
  30.8 30.7 %all-gather.3.cloned.1.call-done = bf16[768,2304]{1,0:T(8,128)(2,1)} async-done(((bf16[48,2304]{1,0:T(8,128)(2,1)}), bf16[768,2304]{1,0:T(8,128)(2,1)}) %all-gather.3.cloned.1.call-update) | async-done | bytes 3538960 | tf_op jit(solution)/shard_map/all_gather | solution.py:179
  61.5 3.1 %convolution_convert_fusion.2 = bf16[256,2304]{1,0:T(8,128)(2,1)S(1)} fusion(bf16[256,768]{1,0:T(8,128)(2,1)S(1)} %bitcast.250, bf16[768,2304]{1,0:T(8,128)(2,1)} %all-gather.3.cloned.1.call-done), kind=kOutput, calls=%fused_computation.105 | convolution fusion | flops 906559488 | bytes 5111808 | tf_op jit(solution)/shard_map/dot_general | solution.py:82
  65.9 6.7 %while.22 = (s32[]{:T(128)}, bf16[3,1,256,4,64]{2,4,3,1,0:T(8,128)(2,1)S(1)}, s32[3]{0:T(128)S(1)}, bf16[1,256,12,3,64]{1,4,2,3,0:T(8,128)(2,1)S(1)}, f32[12]{0:...) while((s32[]{:T(128)}, ...), condition=%wide.region_4.5_spmd.clone, body=%wide.region_0.4_spmd.clone.sunk | while | flops 69076232 | bytes 4099327 | solution.py:97
  72.6 28.5 %all-gather.5.cloned.1.call-done = bf16[768,768]{0,1:T(8,128)(2,1)} async-done(((bf16[768,48]{0,1:T(8,128)(2,1)}), bf16[768,768]{0,1:T(8,128)(2,1)}) %all-gather.5.cloned.1.call-update) | async-done | bytes 1179664 | tf_op jit(solution)/shard_map/all_gather | solution.py:180
  101.1 1.9 %fusion.127 = (f32[256]{0:T(256)S(1)}, f32[256,768]{1,0:T(8,128)S(1)}) fusion(bf16[256,768]{0,1:T(8,128)(2,1)S(1)} %bitcast.248, bf16[768,768]{0,1:T(8,128)(2,1)} %all-gather.5.cloned.1.call-done), kind=kOutput, calls=%fused_computation.175 | convolution fusion | flops 302186240 | bytes 2360320 | tf_op jit(solution)/shard_map/dot_general | solution.py:99
  103.5 1.0 fusion.104
  104.5 1.9 %fusion.128 = f32[768,768]{0,1:T(8,128)} fusion(bf16[256,768]{0,1:T(8,128)(2,1)S(1)} %bitcast.249, bf16[256,768]{1,0:T(8,128)(2,1)S(1)} %get-tuple-element.171), kind=kOutput, calls=%fused_computation.176 | convolution fusion | flops 301989888 | bytes 3145728 | tf_op jit(solution)/shard_map/dot_general | solution.py:111
  106.5 1.0 copy-done.5
  109.7 27.6 %while.23 = (s32[]{:T(128)}, bf16[3,1,256,4,3,64]{2,5,4,3,0,1:T(8,128)(2,1)}, s32[3]{0:T(128)S(1)}, bf16[1,256,12,3,64]{1,4,2,3,0:T(8,128)(2,1)S(1)}, f32[12]{0:...) while((s32[]{:T(128)}, ...), condition=%wide.region_16.17_spmd.clone, body=%wide.region_9.16_spmd.clone.sunk | while | flops 174458624 | bytes 15942179 | solution.py:151
  111.8 1.3 fusion.177
  113.5 2.4 %fusion.178 = (f32[256,4]{0,1:T(4,128)S(1)}, f32[256,4]{0,1:T(4,128)}, f32[1,256,4,64]{1,3,2,0:T(8,128)}) fusion(f32[256,4]{0,1:T(4,128)S(1)} %get-tuple-element.301, bf16[1,256,12,3,64]{1,4,2,3,0:T(8,128)(2,1)S(1)} %get-tuple-element.372, s32[]{:T(128)S(6)} %select_n.35, f32[1,256,4,64]{1,3,2,0:T(8,128)S(1)} %convolution_bitcast_fusion.3, ...), kind=kOutput, calls=%fused_computation.68.clone.1 | convolution fusion | flops 35585280 | bytes 5134352 | tf_op jit(solution)/shard_map/while/body/eval_jaxpr/whqk,wkhd->wqhd/dot_general | solution.py:45
  115.8 1.1 fusion.179
  116.9 1.2 fusion.176
  121.0 1.3 fusion.177
  122.7 2.4 %fusion.178 = (f32[256,4]{0,1:T(4,128)S(1)}, f32[256,4]{0,1:T(4,128)}, f32[1,256,4,64]{1,3,2,0:T(8,128)}) fusion(f32[256,4]{0,1:T(4,128)S(1)} %get-tuple-element.301, bf16[1,256,12,3,64]{1,4,2,3,0:T(8,128)(2,1)S(1)} %get-tuple-element.372, s32[]{:T(128)S(6)} %select_n.35, f32[1,256,4,64]{1,3,2,0:T(8,128)S(1)} %convolution_bitcast_fusion.3, ...), kind=kOutput, calls=%fused_computation.68.clone.1 | convolution fusion | flops 35585280 | bytes 5134352 | tf_op jit(solution)/shard_map/while/body/eval_jaxpr/whqk,wkhd->wqhd/dot_general | solution.py:45
  125.0 1.1 fusion.179
  126.1 1.2 fusion.176
  130.2 1.3 fusion.177
  131.9 2.4 %fusion.178 = (f32[256,4]{0,1:T(4,128)S(1)}, f32[256,4]{0,1:T(4,128)}, f32[1,256,4,64]{1,3,2,0:T(8,128)}) fusion(f32[256,4]{0,1:T(4,128)S(1)} %get-tuple-element.301, bf16[1,256,12,3,64]{1,4,2,3,0:T(8,128)(2,1)S(1)} %get-tuple-element.372, s32[]{:T(128)S(6)} %select_n.35, f32[1,256,4,64]{1,3,2,0:T(8,128)S(1)} %convolution_bitcast_fusion.3, ...), kind=kOutput, calls=%fused_computation.68.clone.1 | convolution fusion | flops 35585280 | bytes 5134352 | tf_op jit(solution)/shard_map/while/body/eval_jaxpr/whqk,wkhd->wqhd/dot_general | solution.py:45
  134.2 1.1 fusion.179
  135.3 1.2 fusion.176
  138.3 3.5 %convolution_convert_fusion.3 = bf16[256,768]{1,0:T(8,128)(2,1)S(1)} fusion(bf16[256,2304]{0,1:T(8,128)(2,1)} %bitcast.18, bf16[768,2304]{1,0:T(8,128)(2,1)} %all-gather.3.cloned.1.call-done), kind=kOutput, calls=%fused_computation.106 | convolution fusion | flops 906166272 | bytes 5111808 | tf_op jit(solution)/shard_map/dot_general | solution.py:155
  142.2 1.5 collective-permute-done.2
  145.3 13.8 %collective-permute-done.3 = bf16[2,4,8,4,768]{4,3,2,1,0:T(4,128)(2,1)S(1)} collective-permute-done((bf16[2,4,8,4,768]{4,3,2,1,0:T(4,128)(2,1)S(1)}, bf16[2,4,8,4,768]{4,3,2,1,0:T(4,128)(2,1)S(1)}, u32[]{:S(2)}, u32[]{:S(2)}) %collective-permute-start.3) | collective-permute-done | bytes 393248 | tf_op jit(solution)/shard_map/ppermute | solution.py:20
  159.2 1.0 add_convert_fusion
  160.2 1.0 add_convert_fusion.1
  161.2 8.0 %reduce-scatter.2.cloned.1.call-done = f32[768,48]{0,1:T(8,128)} async-done(((f32[768,768]{0,1:T(8,128)}), f32[768,48]{0,1:T(8,128)}) %reduce-scatter.2.cloned.1.call-update) | async-done | bytes 147472 | tf_op jit(solution)/shard_map/reduce_scatter | solution.py:204
  169.2 1.6 broadcast_multiply_fusion
  (144 shorter events, 21.8 us)
Async XLA Ops:
  7.2 54.3 %all-gather.3.cloned.1.call-start = ((), (), s32[]{:S(2)}) async-start(), calls=%async_computation.1 | async-start | bytes 3760128 | tf_op jit(solution)/shard_map/all_gather | solution.py:179
  7.9 93.2 %all-gather.5.cloned.1.call-start = ((), (), s32[]{:S(2)}) async-start(), calls=%async_computation.2 | async-start | bytes 1253376 | tf_op jit(solution)/shard_map/all_gather | solution.py:180
  10.0 18.1 %collective-permute-start = (bf16[2,4,8,4,768]{4,3,2,1,0:T(4,128)(2,1)S(1)}, bf16[2,4,8,4,768]{4,3,2,1,0:T(4,128)(2,1)S(1)}, u32[]{:S(2)}, u32[]{:S(2)}) collective-permute-start(bf16[2,4,8,4,768]{4,3,2,1,0:T(4,128)(2,1)S(1)} %pad_maximum_fusion.5), channel_id=1, source_target_pairs={{0,14},{2,0},{4,2},{6,4},{8,6},{10,8},{12,10},{14,12},{1,15},{3,1}... | collective-permute-start | bytes 1179656 | tf_op jit(solution)/shard_map/ppermute | solution.py:20
  28.2 0.7 copy-start.6
  28.5 1.8 %collective-permute-start.1 = (bf16[2,4,4,8,768]{4,3,2,1,0:T(8,128)(2,1)S(1)}, bf16[2,4,4,8,768]{4,3,2,1,0:T(8,128)(2,1)S(1)}, u32[]{:S(2)}, u32[]{:S(2)}) collective-permute-start(bf16[2,4,4,8,768]{4,3,2,1,0:T(8,128)(2,1)S(1)} %pad_maximum_fusion.6), channel_id=1, source_target_pairs={{0,1},{1,0},{2,3},{3,2},{4,5},{5,4},{6,7},{7,6},{8,9},{9,8},{10,11... | collective-permute-start | bytes 1179656 | tf_op jit(solution)/shard_map/ppermute | solution.py:20
  28.6 140.6 %reduce-scatter.2.cloned.1.call-start = ((), (), s32[]{:S(2)}) async-start(), calls=%async_computation.3 | async-start | bytes 2506752 | tf_op jit(solution)/shard_map/reduce_scatter | solution.py:204
  65.2 0.7 copy-start.7
  106.5 1.0 copy-start.5
  106.5 1.8 %copy-start = (bf16[768,768]{0,1:T(8,128)(2,1)S(1)}, bf16[768,768]{0,1:T(8,128)(2,1)}, u32[]{:S(2)}) copy-start(bf16[768,768]{0,1:T(8,128)(2,1)} %all-gather.5.cloned.1.call-done) | copy-start | bytes 3538948
  109.7 1.3 copy-start.10
  109.7 2.1 %copy-start.8 = (f32[12]{0:T(128)}, f32[12]{0:T(128)S(1)}, u32[]{:S(2)}) copy-start(f32[12]{0:T(128)S(1)} %get-tuple-element.373) | copy-start | bytes 148 | tf_op jit(solution)/shard_map/while
  111.1 0.6 copy-start.12
  111.8 1.3 copy-start.13
  116.9 2.0 %copy-start.9 = (f32[12]{0:T(128)S(1)}, f32[12]{0:T(128)}, u32[]{:S(2)}) copy-start(f32[12]{0:T(128)} %copy-done.8) | copy-start | bytes 148 | tf_op jit(solution)/shard_map/while
  116.9 2.0 %copy-start.11 = (s32[3]{0:T(128)S(1)}, s32[3]{0:T(128)}, u32[]{:S(2)}) copy-start(s32[3]{0:T(128)} %copy-done.10) | copy-start | bytes 40 | tf_op jit(solution)/shard_map/while
  118.9 1.3 copy-start.10
  118.9 2.1 %copy-start.8 = (f32[12]{0:T(128)}, f32[12]{0:T(128)S(1)}, u32[]{:S(2)}) copy-start(f32[12]{0:T(128)S(1)} %get-tuple-element.373) | copy-start | bytes 148 | tf_op jit(solution)/shard_map/while
  121.0 1.3 copy-start.13
  126.1 2.0 %copy-start.9 = (f32[12]{0:T(128)S(1)}, f32[12]{0:T(128)}, u32[]{:S(2)}) copy-start(f32[12]{0:T(128)} %copy-done.8) | copy-start | bytes 148 | tf_op jit(solution)/shard_map/while
  126.1 2.0 %copy-start.11 = (s32[3]{0:T(128)S(1)}, s32[3]{0:T(128)}, u32[]{:S(2)}) copy-start(s32[3]{0:T(128)} %copy-done.10) | copy-start | bytes 40 | tf_op jit(solution)/shard_map/while
  128.1 1.3 copy-start.10
  128.1 2.1 %copy-start.8 = (f32[12]{0:T(128)}, f32[12]{0:T(128)S(1)}, u32[]{:S(2)}) copy-start(f32[12]{0:T(128)S(1)} %get-tuple-element.373) | copy-start | bytes 148 | tf_op jit(solution)/shard_map/while
  129.5 0.7 copy-start.12
  130.2 1.3 copy-start.13
  135.3 2.0 %copy-start.9 = (f32[12]{0:T(128)S(1)}, f32[12]{0:T(128)}, u32[]{:S(2)}) copy-start(f32[12]{0:T(128)} %copy-done.8) | copy-start | bytes 148 | tf_op jit(solution)/shard_map/while
  135.3 2.0 %copy-start.11 = (s32[3]{0:T(128)S(1)}, s32[3]{0:T(128)}, u32[]{:S(2)}) copy-start(s32[3]{0:T(128)} %copy-done.10) | copy-start | bytes 40 | tf_op jit(solution)/shard_map/while
  141.8 1.9 %copy-start.1 = (bf16[128,768]{1,0:T(8,128)(2,1)S(1)}, bf16[128,768]{1,0:T(8,128)(2,1)}, u32[]{:S(2)}) copy-start(bf16[128,768]{1,0:T(8,128)(2,1)} %get-tuple-element.187) | copy-start | bytes 589828
  141.8 1.9 %copy-start.2 = (bf16[128,768]{1,0:T(8,128)(2,1)S(1)}, bf16[128,768]{1,0:T(8,128)(2,1)}, u32[]{:S(2)}) copy-start(bf16[128,768]{1,0:T(8,128)(2,1)} %get-tuple-element.188) | copy-start | bytes 589828
  141.9 1.8 %collective-permute-start.2 = (bf16[2,4,4,8,768]{4,3,2,1,0:T(8,128)(2,1)S(1)}, bf16[2,4,4,8,768]{4,3,2,1,0:T(8,128)(2,1)S(1)}, u32[]{:S(2)}, u32[]{:S(2)}) collective-permute-start(bf16[2,4,4,8,768]{4,3,2,1,0:T(8,128)(2,1)S(1)} %pad_maximum_fusion.8), channel_id=1, source_target_pairs={{0,1},{1,0},{2,3},{3,2},{4,5},{5,4},{6,7},{7,6},{8,9},{9,8},{10,11... | collective-permute-start | bytes 1179656 | tf_op jit(solution)/shard_map/ppermute | solution.py:20
  144.0 15.2 %copy-start.3 = (bf16[4,8,8,768]{3,2,1,0:T(8,128)(2,1)S(1)}, bf16[4,8,8,768]{3,2,1,0:T(8,128)(2,1)}, u32[]{:S(2)}) copy-start(bf16[4,8,8,768]{3,2,1,0:T(8,128)(2,1)} %param.11) | copy-start | bytes 1179652
  144.4 15.8 %copy-start.4 = (bf16[4,8,8,768]{3,2,1,0:T(8,128)(2,1)S(1)}, bf16[4,8,8,768]{3,2,1,0:T(8,128)(2,1)}, u32[]{:S(2)}) copy-start(bf16[4,8,8,768]{3,2,1,0:T(8,128)(2,1)} %param.10) | copy-start | bytes 1179652
  144.4 14.6 %collective-permute-start.3 = (bf16[2,4,8,4,768]{4,3,2,1,0:T(4,128)(2,1)S(1)}, bf16[2,4,8,4,768]{4,3,2,1,0:T(4,128)(2,1)S(1)}, u32[]{:S(2)}, u32[]{:S(2)}) collective-permute-start(bf16[2,4,8,4,768]{4,3,2,1,0:T(4,128)(2,1)S(1)} %pad_maximum_fusion.9), channel_id=1, source_target_pairs={{0,2},{2,4},{4,6},{6,8},{8,10},{10,12},{12,14},{14,0},{1,3},{3,5},... | collective-permute-start | bytes 1179656 | tf_op jit(solution)/shard_map/ppermute | solution.py:20
  (1 other events, 0.6 us)
Sparse Core Ops, SparseCore 0:
  10.3 51.1 all-gather.2
  63.8 37.3 all-gather.4
  106.6 62.5 reduce-scatter.1
where the time goes:
time: 178 us; the launch traced here: 177 us
  waiting for transfers between devices  96.5 us (54%)
  matrix products  30.1 us (17%)
  other arithmetic  14.1 us (8%)
  between operations  14.1 us (8%)
  local copies, waits for them, and re-layouts  10.8 us (6%)
  starting transfers between devices  7.41 us (4%)
  loops' own time  4.36 us (2%)
    all_gather x1, waiting for transfers between devices, shards(): lax.all_gather(qkv_weight, ('space', 'dp'), axis=0, tiled=True)  30.7 us
    ppermute x4, waiting for transfers between devices, shifted_2(): return lax.ppermute(value, axis, pairs)  28.6 us
    all_gather x1, waiting for transfers between devices, shards(): lax.all_gather(proj_weight, ('space', 'dp'), axis=1, tiled=True)  28.5 us
    dot_general x18, matrix products, product(): jnp.einsum(pattern, left_side, right_side, preferred_element_type=jnp.flo...  17.7 us
    reduce_scatter x1, waiting for transfers between devices, shards(): lax.psum_scatter(proj_term, ('space', 'dp'), scatter_dimension=1, tiled=T...  8.02 us
    ppermute x4, starting transfers between devices, shifted_2(): return lax.ppermute(value, axis, pairs)  7.29 us
  transfers between devices with their start and end apart: 7, of which 7 were waited for; matrix products, arithmetic and copies ran while one was open for 26% of the time, Pallas kernels for 0%

commit v1 on v0

--- a/solution.py
+++ b/solution.py
@@ -1,8 +1,11 @@
+import functools
 import math
 
 import jax
 import jax.numpy as jnp
 from jax import lax
+from jax.experimental import pallas as pl
+from jax.experimental.pallas import tpu as pltpu
 from jax.sharding import PartitionSpec as P
 
 HEAD_GROUP = 4
@@ -209,6 +212,340 @@
     return (block_output, token_grad, proj_grad)
 
 
+MESH = pl.DeviceIdType.MESH
+F32 = jnp.float32
+BF16 = jnp.bfloat16
+PIECES = 4
+
+
+def dot_nn(a, b):
+    return lax.dot_general(a, b, (((1,), (0,)), ((), ())), preferred_element_type=F32)
+
+
+def dot_nt(a, b):
+    return lax.dot_general(a, b, (((1,), (1,)), ((), ())), preferred_element_type=F32)
+
+
+def dot_tn(a, b):
+    return lax.dot_general(a, b, (((0,), (0,)), ((), ())), preferred_element_type=F32)
+
+
+def unit_parts(rows):
+    wide = rows.astype(F32)
+    inv = lax.rsqrt(jnp.sum(wide * wide, axis=-1, keepdims=True) + 1e-06)
+    unit = wide * inv
+    return unit, inv, unit.astype(BF16)
+
+
+def slab_kernel(
+    nz, heads, size, scale_out,
+    scales, fields, region, own,
+    out, pgrad,
+    w, halo, back, packed, prob, att, gatt, gpacked, allowed_ref,
+    gsend, grecv, hsend, hrecv, zsend, zrecv,
+    send_sems, recv_sems,
+):
+    y, s, c = lax.axis_index("groups"), lax.axis_index("space"), lax.axis_index("dp")
+    ns = nz * 2
+    z, x = s // 2, s % 2
+    chans = own.shape[-1]
+    half_w = chans // 2
+
+    def dev(yy, ss, cc):
+        return {"groups": yy, "space": ss, "dp": cc}
+
+    x_next = z * 2 + (1 - x)
+    zs = [lax.rem(z + k, nz) for k in range(1, nz)]
+    z_devs = [dev(y, zz * 2 + x, c) for zz in zs]
+    x_dev, y_dev, core_dev = dev(y, x_next, c), dev(1 - y, s, c), dev(y, s, 1 - c)
+    before, after = lax.rem(s + ns - 1, ns), lax.rem(s + 1, ns)
+    barrier = pltpu.get_barrier_semaphore()
+    peers = z_devs + [x_dev, y_dev, core_dev]
+    peers += [dev(y, ss, cc) for ss in (before, after) for cc in (c, 1 - c)]
+    for peer in peers:
+        pl.semaphore_signal(barrier, inc=1, device_id=peer, device_id_type=MESH)
+    pl.semaphore_wait(barrier, len(peers))
+
+    made = []
+
+    def copy(src, dst, where):
+        index = len(made)
+        made.append(
+            pltpu.make_async_remote_copy(
+                src_ref=src, dst_ref=dst, send_sem=send_sems.at[index],
+                recv_sem=recv_sems.at[index], device_id=where, device_id_type=MESH,
+            )
+        )
+        return made[-1]
+
+    def lanes(which):
+        return pl.ds(pl.multiple_of(which * half_w, 128), half_w)
+
+    def goes(q):
+        hi, wi = q // 2, q % 2
+        return dev(y, s if wi else before, c if hi else 1 - c)
+
+    def came(q):
+        hi, wi = q // 2, q % 2
+        return dev(y, s if wi else after, c if hi else 1 - c)
+
+    halos = [[copy(fields.at[f, q], halo.at[f, q], goes(q)) for q in range(3)] for f in range(2)]
+    mine, other = lanes(y), lanes(1 - y)
+    first_y = c == 0
+    s_a, y_a = jnp.where(first_y, s, x_next), jnp.where(first_y, 1 - y, y)
+    s_b, y_b = jnp.where(first_y, x_next, s), jnp.where(first_y, y, 1 - y)
+    a_dev, b_dev = dev(y_a, s_a, c), dev(y_b, s_b, c)
+    x_a = jnp.where(first_y, x, 1 - x)
+    got_a = lanes(y_a)
+    st1 = [
+        [copy(own.at[p, :, mine], w.at[p, z, x, c, :, mine], zd) for zd in z_devs]
+        for p in range(PIECES)
+    ]
+    st2, st3a, st3b, st4 = [], [], [], []
+    for p in range(PIECES):
+        quarter = w.at[p, :, x, c, :, mine]
+        st2.append(copy(quarter, quarter, a_dev))
+        st3a.append(copy(quarter, quarter, b_dev))
+        second = w.at[p, :, x_a, c, :, got_a]
+        st3b.append(copy(second, second, b_dev))
+        whole = w.at[p, :, :, c]
+        st4.append(copy(whole, whole, core_dev))
+
+    def step1(p):
+        for item in st1[p]:
+            item.wait_recv()
+        st2[p].start()
+        st3a[p].start()
+
+    def step2(p):
+        st2[p].wait_recv()
+        st3b[p].start()
+
+    def step3(p):
+        st3a[p].wait_recv()
+        st3b[p].wait_recv()
+        st4[p].start()
+
+    for item in halos[0]:
+        item.start()
+    for p in range(PIECES):
+        for item in st1[p]:
+            item.start()
+        if p == 1:
+            for item in halos[1]:
+                item.start()
+    for p in range(PIECES):
+        w[p, z, x, c, :, mine] = own[p, :, mine]
+    labels = jnp.broadcast_to(region[...], (region.shape[1], region.shape[1]))
+    allowed_ref[...] = jnp.where(labels == labels.T, 1.0, 0.0)
+
+    step1(0)
+    step1(1)
+    step2(0)
+    step1(2)
+    step2(1)
+    step3(0)
+    step1(3)
+    step2(2)
+    step3(1)
+
+    def window(f):
+        for item in halos[f]:
+            item.wait_recv()
+        return jnp.concatenate([halo[f, 0], halo[f, 1], halo[f, 2], fields[f, 3]], axis=0)
+
+    per_piece = heads // 3
+    pairs = per_piece // 2
+
+    def weight(p):
+        return w[p].reshape(-1, chans)
+
+    def forward(p, rows):
+        st4[p].wait_recv()
+        packed[p] = dot_nn(rows, weight(p)).astype(BF16)
+
+        @pl.loop(0, pairs)
+        def _(pair):
+            piece = packed[p, :, pl.ds(pl.multiple_of(pair * 6 * size, 128), 6 * size)]
+            outs = []
+            for i in range(2):
+                head = p * per_piece + pair * 2 + i
+                q, k, v = [piece[:, (3 * i + j) * size:(3 * i + j + 1) * size] for j in range(3)]
+                q_low, k_low = unit_parts(q)[2], unit_parts(k)[2]
+                scores = dot_nt(q_low, k_low) * scales[head]
+                raised = jnp.exp(scores) * allowed_ref[...]
+                probability = raised / jnp.sum(raised, axis=-1, keepdims=True)
+                prob[head] = probability
+                outs.append(dot_nn(probability.astype(BF16), v).astype(BF16))
+            at = p * per_piece * size + pair * 2 * size
+            att[:, pl.ds(pl.multiple_of(at, 128), 2 * size)] = jnp.concatenate(outs, axis=1)
+
+    rows = window(0)
+    forward(0, rows)
+    step2(3)
+    step3(2)
+    forward(1, rows)
+    step3(3)
+    forward(2, rows)
+    st4[3].wait_recv()
+
+    attended = att[...]
+    mixed = dot_nt(attended, weight(3))
+    centered = mixed - jnp.mean(mixed, axis=-1, keepdims=True)
+    inv_dev = lax.rsqrt(jnp.mean(centered * centered, axis=-1, keepdims=True) + 1e-05)
+    normed = centered * inv_dev
+    result = (rows.astype(F32) + normed.astype(BF16).astype(F32)).astype(BF16)
+    quad = out.shape[2]
+    returns = [[copy(back.at[f, q], out.at[f, q], came(q)) for q in range(3)] for f in range(2)]
+    for q in range(3):
+        back[0, q] = result[q * quad:(q + 1) * quad]
+        returns[0][q].start()
+    out[0, 3] = result[3 * quad:]
+    grad_in = window(1).astype(F32)
+    grad_low = (
+        inv_dev
+        * (
+            grad_in
+            - jnp.mean(grad_in, axis=-1, keepdims=True)
+            - normed * jnp.mean(grad_in * normed, axis=-1, keepdims=True)
+        )
+    ).astype(BF16)
+    gsend[...] = dot_tn(grad_low, attended).astype(BF16).reshape(gsend.shape)
+    to_core = copy(gsend.at[:, :, 1 - c], grecv, core_dev)
+    to_core.start()
+    gatt[...] = dot_nn(grad_low, weight(3)).astype(BF16)
+
+    def backward(p):
+        @pl.loop(0, pairs)
+        def _(pair):
+            at = pl.ds(pl.multiple_of(pair * 6 * size, 128), 6 * size)
+            piece = packed[p, :, at]
+            g_at = p * per_piece * size + pair * 2 * size
+            g_pair = gatt[:, pl.ds(pl.multiple_of(g_at, 128), 2 * size)]
+            outs = []
+            for i in range(2):
+                head = p * per_piece + pair * 2 + i
+                q, k, v = [piece[:, (3 * i + j) * size:(3 * i + j + 1) * size] for j in range(3)]
+                q_unit, q_inv, q_low = unit_parts(q)
+                k_unit, k_inv, k_low = unit_parts(k)
+                g = g_pair[:, i * size:(i + 1) * size]
+                probability = prob[head]
+                g_prob = dot_nt(g, v)
+                g_val = dot_tn(probability.astype(BF16), g)
+                inner = jnp.sum(probability * g_prob, axis=-1, keepdims=True)
+                scaled = (probability * (g_prob - inner) * scales[head]).astype(BF16)
+                g_q = dot_nn(scaled, k_low)
+                g_k = dot_tn(scaled, q_low)
+                g_q = q_inv * (g_q - q_unit * jnp.sum(g_q * q_unit, axis=-1, keepdims=True))
+                g_k = k_inv * (g_k - k_unit * jnp.sum(g_k * k_unit, axis=-1, keepdims=True))
+                outs += [g_q.astype(BF16), g_k.astype(BF16), g_val.astype(BF16)]
+            gpacked[p, :, at] = jnp.concatenate(outs, axis=1)
+
+    backward(0)
+    to_core.wait_recv()
+    hsend[...] = (gsend[:, :, c].astype(F32) + grecv[...].astype(F32)).astype(BF16)
+    to_x = copy(hsend.at[:, 1 - x], hrecv, x_dev)
+    to_x.start()
+    backward(1)
+    to_x.wait_recv()
+    zsend[...] = (hsend[:, x].astype(F32) + hrecv[...].astype(F32)).astype(BF16)
+    to_z = [copy(zsend.at[zz], zrecv.at[k], zd) for k, (zz, zd) in enumerate(zip(zs, z_devs))]
+    for item in to_z:
+        item.start()
+    backward(2)
+    grad_rows = dot_nt(gpacked[0], weight(0))
+    grad_rows += dot_nt(gpacked[1], weight(1))
+    grad_rows += dot_nt(gpacked[2], weight(2))
+    grad_out = (grad_in + grad_rows.astype(BF16).astype(F32)).astype(BF16)
+    for q in range(3):
+        back[1, q] = grad_out[q * quad:(q + 1) * quad]
+        returns[1][q].start()
+    out[1, 3] = grad_out[3 * quad:]
+    total = zsend[z].astype(F32)
+    for k, item in enumerate(to_z):
+        item.wait_recv()
+        total += zrecv[k].astype(F32)
+    pgrad[...] = total * scale_out
+    for item in returns[0] + returns[1]:
+        item.wait_recv()
+    for item in made:
+        item.wait_send()
+
+
+def to_quads(field):
+    lead = field.shape[0]
+    rest = tuple(field.shape[4:])
+    d, h, wd = field.shape[1:4]
+    split = field.reshape((lead, d, 2, h // 2, 2, wd // 2) + rest)
+    order = (0, 2, 4, 1, 3, 5) + tuple(range(6, 6 + len(rest)))
+    return split.transpose(order).reshape((lead, 4, d * h * wd // 4) + rest)
+
+
+def from_quads(quads, d, h, wd):
+    lead, chans = quads.shape[0], quads.shape[-1]
+    split = quads.reshape(lead, 2, 2, d, h // 2, wd // 2, chans)
+    return split.transpose(0, 3, 1, 4, 2, 5, 6).reshape(lead, d, h, wd, chans)
+
+
+def fused_shards(tokens, cotangent, region, qkv_weight, proj_weight, logit_scale):
+    d, h, wd, chans = tokens.shape
+    heads = logit_scale.shape[0]
+    space = lax.axis_size("space")
+    nz = space // 2
+    count = d * h * wd
+    share = qkv_weight.shape[0]
+    fields = to_quads(jnp.stack([tokens, cotangent]))
+    labels = to_quads(jnp.roll(region, (SD, SH, SW), axis=(0, 1, 2))[None])
+    labels = labels.astype(F32).reshape(1, count)
+    own = jnp.concatenate(
+        [qkv_weight.reshape(share, 3, chans).transpose(1, 0, 2), proj_weight.T[None]], axis=0
+    )
+    copies = 6 + PIECES * (nz - 1) + 4 * PIECES + 6 + 2 + nz - 1
+    vmem = pl.BlockSpec(memory_space=pltpu.VMEM)
+    scale_out = 1.0 / math.sqrt(count * space * lax.axis_size("dp"))
+    out, pgrad = pl.pallas_call(
+        functools.partial(slab_kernel, nz, heads, chans // heads, scale_out),
+        out_shape=[
+            jax.ShapeDtypeStruct(fields.shape, BF16),
+            jax.ShapeDtypeStruct((share, chans), F32),
+        ],
+        in_specs=[pl.BlockSpec(memory_space=pltpu.SMEM), vmem, vmem, vmem],
+        out_specs=[vmem, vmem],
+        scratch_shapes=[
+            pltpu.VMEM((PIECES, nz, 2, 2, share, chans), BF16),
+            pltpu.VMEM((2, 3, count // 4, chans), BF16),
+            pltpu.VMEM((2, 3, count // 4, chans), BF16),
+            pltpu.VMEM((3, count, chans), BF16),
+            pltpu.VMEM((heads, count, count), F32),
+            pltpu.VMEM((count, chans), BF16),
+            pltpu.VMEM((count, chans), BF16),
+            pltpu.VMEM((3, count, chans), BF16),
+            pltpu.VMEM((count, count), F32),
+            pltpu.VMEM((nz, 2, 2, share, chans), BF16),
+            pltpu.VMEM((nz, 2, share, chans), BF16),
+            pltpu.VMEM((nz, 2, share, chans), BF16),
+            pltpu.VMEM((nz, share, chans), BF16),
+            pltpu.VMEM((nz, share, chans), BF16),
+            pltpu.VMEM((nz - 1, share, chans), BF16),
+            pltpu.SemaphoreType.DMA((copies,)),
+            pltpu.SemaphoreType.DMA((copies,)),
+        ],
+        compiler_params=pltpu.CompilerParams(
+            collective_id=0, has_side_effects=True, vmem_limit_bytes=48 * 1024 * 1024
+        ),
+    )(logit_scale, fields, labels, own)
+    grids = from_quads(out, d, h, wd)
+    return (grids[0], grids[1], pgrad.T)
+
+
+def block(tokens, cotangent, region, qkv_weight, proj_weight, logit_scale):
+    sizes = [lax.axis_size(axis) for axis in ("groups", "space", "dp")]
+    share = qkv_weight.shape[0]
+    fits = sizes[0] == 2 and sizes[2] == 2 and sizes[1] % 2 == 0 and sizes[1] >= 4
+    body = fused_shards if fits and share % 16 == 0 and tokens.shape[0] == WD else shards
+    return body(tokens, cotangent, region, qkv_weight, proj_weight, logit_scale)
+
+
 def solution(mesh):
     in_specs = (
         P("groups", "dp", "space", None),
@@ -223,4 +560,6 @@
         P("groups", "dp", "space", None),
         P("groups", ("space", "dp")),
     )
-    return jax.shard_map(shards, mesh=mesh, in_specs=in_specs, out_specs=out_specs, check_vma=False)
+    return jax.shard_map(
+        block, mesh=mesh, in_specs=in_specs, out_specs=out_specs, check_vma=False
+    )

time: 178 us -> 78.7 us (0.44)
  waiting for transfers between devices: 96.5 us -> 0 us
  Pallas kernels: 0 us -> 70.4 us
  matrix products: 30.1 us -> 0 us
  other arithmetic: 14.1 us -> 0.55 us
  between operations: 14.1 us -> 0.76 us
  starting transfers between devices: 7.41 us -> 0 us
  loops' own time: 4.36 us -> 0 us
  local copies, waits for them, and re-layouts: 10.8 us -> 6.77 us
    pallas_call x0 -> x1, Pallas kernels: none -> 70.4 us  [fused_shards(): pl.pallas_call(functools.partial(slab_kernel, nz, heads, chans // heads,...]
    all_gather x2 -> x0, waiting for transfers between devices: 59.2 us -> none  [the longest x1 30.7 us: shards(): lax.all_gather(qkv_weight, ('space', 'dp'), axis=0, tiled=True)]
    ppermute x4 -> x0, waiting for transfers between devices: 28.6 us -> none  [shifted_2(): return lax.ppermute(value, axis, pairs)]
    dot_general x23 -> x0, matrix products: 28.6 us -> none  [the longest x18 17.7 us: product(): jnp.einsum(pattern, left_side, right_side, preferred_element_type=jnp.flo...]
    reduce_scatter x1 -> x0, waiting for transfers between devices: 8.02 us -> none  [shards(): lax.psum_scatter(proj_term, ('space', 'dp'), scatter_dimension=1, tiled=T...]
    ppermute x4 -> x0, starting transfers between devices: 7.29 us -> none  [shifted_2(): return lax.ppermute(value, axis, pairs)]
    another operation x10 -> x0, other arithmetic: 4.89 us -> none  [the longest x3 3.17 us: backward_group(): jnp.stack([grad_query, grad_key, grad_values], axis=3).astype(jnp.bfloat16)]
    another operation x2 -> x0, loops' own time: 4.36 us -> none  [the longest x1 2.28 us: window_block(): grad_packed = lax.map(backward_group, group_ids)]
  transfers between devices with their start and end apart: 7 -> 0, of which waited for: 7 -> 0; matrix products, arithmetic and copies ran while one was open for 26% -> 0% of each run, Pallas kernels for 0% -> 0%
where the time goes in v1:
time: 78.7 us; the launch traced here: 78.5 us
  Pallas kernels  70.4 us (89%)
  local copies, waits for them, and re-layouts  6.77 us (9%)
    pallas_call x1, Pallas kernels, fused_shards(): pl.pallas_call(functools.partial(slab_kernel, nz, heads, chans // heads,...  70.4 us
    unnamed x11, local copies, waits for them, and re-layouts  3 us
    squeeze x2, local copies, waits for them, and re-layouts, fused_shards(): return (grids[0], grids[1], pgrad.T)  1.68 us

profile of v1, /device:TPU:0, one launch (start us, length us, event | category | flops | bytes accessed | tf_op | source)
XLA Modules:
  0.0 78.5 jit_solution(1605296709652874904)
XLA Ops:
  0.6 0.0 copy-start.3
  0.6 0.8 fusion.2
  1.4 0.1 slice_add_fusion
  1.5 0.1 add_convert_fusion
  1.6 0.1 convert_element_type.22
  1.7 0.1 convert_element_type.24.region
  1.8 0.0 copy-done.3
  1.8 0.0 copy-start.4
  1.8 0.0 copy-start.1
  1.9 0.8 %copy-done.4 = bf16[768,48]{0,1:T(8,128)(2,1)S(1)} copy-done((bf16[768,48]{0,1:T(8,128)(2,1)S(1)}, bf16[768,48]{0,1:T(8,128)(2,1)}, u32[]{:S(2)}) %copy-start.4) | copy-done | bytes 73752
  2.7 0.1 copy-done.1
  2.8 0.0 copy-start.2
  2.8 0.1 stack.9
  2.9 0.9 %copy-done.2 = bf16[4,8,8,768]{3,2,1,0:T(8,128)(2,1)S(1)} copy-done((bf16[4,8,8,768]{3,2,1,0:T(8,128)(2,1)S(1)}, bf16[4,8,8,768]{3,2,1,0:T(8,128)(2,1)}, u32[]{:S(2)}) %copy-start.2) | copy-done | bytes 393240
  3.8 0.1 stack.10
  3.9 0.4 copy_bitcast_fusion
  4.3 0.0 copy-start
  4.3 0.2 reshape.42.fields
  4.5 0.5 copy-done
  5.0 70.4 %shard_map.85 = (bf16[2,4,64,768]{3,2,1,0:T(8,128)(2,1)S(1)}, f32[48,768]{1,0:T(8,128)S(1)}) custom-call(f32[12]{0:T(128)S(1)} %copy-done, bf16[2,4,64,768]{3,2,1,0:T(8,128)(2,1)S(1)} %reshape.42.fields, f32[1,256]{1,0:T(1,128)S(1)} %convert_element_type.24.region, bf16[4,48,768]{2,1,0:T(8,128)(2,1)S(1)} %pad_maximum_fusion.1.own), custom_call_target="tpu_custom_call" | custom-call | tf_op jit(solution)/shard_map/pallas_call | solution.py:506
  75.4 0.2 reshape.44
  75.6 0.3 fusion.1
  75.8 0.1 copy.19
  76.0 0.8 %squeeze.7 = bf16[4,8,8,768]{3,2,1,0:T(8,128)(2,1)} reshape(bf16[1,4,2,4,2,4,768]{6,5,4,3,2,1,0:T(4,128)(2,1)S(1)} %copy.19) | data formatting | bytes 786432 | tf_op jit(solution)/shard_map/squeeze | solution.py:538
  76.8 0.1 copy.18
  77.0 0.8 %squeeze.6 = bf16[4,8,8,768]{3,2,1,0:T(8,128)(2,1)} reshape(bf16[1,4,2,4,2,4,768]{6,5,4,3,2,1,0:T(4,128)(2,1)S(1)} %copy.18) | data formatting | bytes 786432 | tf_op jit(solution)/shard_map/squeeze | solution.py:538
  77.8 0.7 copy.28
  (4 shorter events, 0.1 us)
Async XLA Ops:
  0.6 1.2 %copy-start.3 = (bf16[48,2304]{1,0:T(8,128)(2,1)S(1)}, bf16[48,2304]{1,0:T(8,128)(2,1)}, u32[]{:S(2)}) copy-start(bf16[48,2304]{1,0:T(8,128)(2,1)} %param.9) | copy-start | bytes 663556
  1.8 0.9 %copy-start.4 = (bf16[768,48]{0,1:T(8,128)(2,1)S(1)}, bf16[768,48]{0,1:T(8,128)(2,1)}, u32[]{:S(2)}) copy-start(bf16[768,48]{0,1:T(8,128)(2,1)} %param.10) | copy-start | bytes 221188
  1.8 1.0 %copy-start.1 = (bf16[4,8,8,768]{3,2,1,0:T(8,128)(2,1)S(1)}, bf16[4,8,8,768]{3,2,1,0:T(8,128)(2,1)}, u32[]{:S(2)}) copy-start(bf16[4,8,8,768]{3,2,1,0:T(8,128)(2,1)} %param.6) | copy-start | bytes 1179652
  2.8 1.0 %copy-start.2 = (bf16[4,8,8,768]{3,2,1,0:T(8,128)(2,1)S(1)}, bf16[4,8,8,768]{3,2,1,0:T(8,128)(2,1)}, u32[]{:S(2)}) copy-start(bf16[4,8,8,768]{3,2,1,0:T(8,128)(2,1)} %param.7) | copy-start | bytes 1179652
  4.3 0.7 copy-start

commit v2 on v1

--- a/solution.py
+++ b/solution.py
@@ -216,6 +216,7 @@
 F32 = jnp.float32
 BF16 = jnp.bfloat16
 PIECES = 4
+LOG2E = math.log2(math.e)
 
 
 def dot_nn(a, b):
@@ -290,52 +291,43 @@
         return dev(y, s if wi else after, c if hi else 1 - c)
 
     halos = [[copy(fields.at[f, q], halo.at[f, q], goes(q)) for q in range(3)] for f in range(2)]
-    mine, other = lanes(y), lanes(1 - y)
-    first_y = c == 0
-    s_a, y_a = jnp.where(first_y, s, x_next), jnp.where(first_y, 1 - y, y)
-    s_b, y_b = jnp.where(first_y, x_next, s), jnp.where(first_y, y, 1 - y)
-    a_dev, b_dev = dev(y_a, s_a, c), dev(y_b, s_b, c)
-    x_a = jnp.where(first_y, x, 1 - x)
-    got_a = lanes(y_a)
-    st1 = [
-        [copy(own.at[p, :, mine], w.at[p, z, x, c, :, mine], zd) for zd in z_devs]
-        for p in range(PIECES)
-    ]
-    st2, st3a, st3b, st4 = [], [], [], []
+    mine = lanes(y)
+    froms = [z] + [lax.rem(z + nz - k, nz) for k in range(1, nz)]
+    st1, st2, st3, st3d, st4 = [], [], [], [], []
     for p in range(PIECES):
-        quarter = w.at[p, :, x, c, :, mine]
-        st2.append(copy(quarter, quarter, a_dev))
-        st3a.append(copy(quarter, quarter, b_dev))
-        second = w.at[p, :, x_a, c, :, got_a]
-        st3b.append(copy(second, second, b_dev))
+        st1.append([copy(own.at[p, :, mine], w.at[p, z, x, c, :, mine], zd) for zd in z_devs])
+        quarters = [w.at[p, zf, x, c, :, mine] for zf in froms]
+        st2.append([copy(own.at[p, :, mine], quarters[0], x_dev)])
+        st2[p] += [copy(quarter, quarter, x_dev) for quarter in quarters[1:]]
+        st3.append([copy(quarter, quarter, y_dev) for quarter in quarters[1:]])
+        diagonal = [w.at[p, zf, 1 - x, c, :, mine] for zf in froms]
+        st3d.append([copy(quarter, quarter, y_dev) for quarter in diagonal])
         whole = w.at[p, :, :, c]
         st4.append(copy(whole, whole, core_dev))
 
     def step1(p):
-        for item in st1[p]:
+        for k in range(1, nz):
+            st1[p][k - 1].wait_recv()
+            st2[p][k].start()
+            st3[p][k - 1].start()
+
+    def step2(p):
+        for arriving, onward in zip(st2[p], st3d[p]):
+            arriving.wait_recv()
+            onward.start()
+
+    def step3(p):
+        for item in st3[p] + st3d[p]:
             item.wait_recv()
-        st2[p].start()
-        st3a[p].start()
-
-    def step2(p):
-        st2[p].wait_recv()
-        st3b[p].start()
-
-    def step3(p):
-        st3a[p].wait_recv()
-        st3b[p].wait_recv()
         st4[p].start()
 
     for item in halos[0]:
         item.start()
     for p in range(PIECES):
-        for item in st1[p]:
+        for item in [st2[p][0]] + st1[p]:
             item.start()
-        if p == 1:
-            for item in halos[1]:
-                item.start()
     for p in range(PIECES):
-        w[p, z, x, c, :, mine] = own[p, :, mine]
+        w[p, z, x, c] = own[p]
     labels = jnp.broadcast_to(region[...], (region.shape[1], region.shape[1]))
     allowed_ref[...] = jnp.where(labels == labels.T, 1.0, 0.0)
 
@@ -346,8 +338,8 @@
     step2(1)
     step3(0)
     step1(3)
-    step2(2)
-    step3(1)
+    for item in halos[1]:
+        item.start()
 
     def window(f):
         for item in halos[f]:
@@ -360,33 +352,33 @@
     def weight(p):
         return w[p].reshape(-1, chans)
 
-    def forward(p, rows):
+    def forward(p, rows, between):
         st4[p].wait_recv()
         packed[p] = dot_nn(rows, weight(p)).astype(BF16)
 
-        @pl.loop(0, pairs)
-        def _(pair):
-            piece = packed[p, :, pl.ds(pl.multiple_of(pair * 6 * size, 128), 6 * size)]
+        for pair in range(pairs):
+            if pair == pairs // 2:
+                between()
+            piece = packed[p, :, pair * 6 * size:(pair + 1) * 6 * size]
             outs = []
             for i in range(2):
                 head = p * per_piece + pair * 2 + i
                 q, k, v = [piece[:, (3 * i + j) * size:(3 * i + j + 1) * size] for j in range(3)]
                 q_low, k_low = unit_parts(q)[2], unit_parts(k)[2]
-                scores = dot_nt(q_low, k_low) * scales[head]
-                raised = jnp.exp(scores) * allowed_ref[...]
-                probability = raised / jnp.sum(raised, axis=-1, keepdims=True)
+                scores = dot_nt(q_low, k_low) * (scales[head] * LOG2E)
+                raised = jnp.exp2(scores) * allowed_ref[...]
+                probability = raised * (1.0 / jnp.sum(raised, axis=-1, keepdims=True))
                 prob[head] = probability
                 outs.append(dot_nn(probability.astype(BF16), v).astype(BF16))
             at = p * per_piece * size + pair * 2 * size
-            att[:, pl.ds(pl.multiple_of(at, 128), 2 * size)] = jnp.concatenate(outs, axis=1)
+            att[:, at:at + 2 * size] = jnp.concatenate(outs, axis=1)
 
     rows = window(0)
-    forward(0, rows)
-    step2(3)
+    forward(0, rows, lambda: step2(2))
+    step3(1)
+    forward(1, rows, lambda: step2(3))
     step3(2)
-    forward(1, rows)
-    step3(3)
-    forward(2, rows)
+    forward(2, rows, lambda: step3(3))
     st4[3].wait_recv()
 
     attended = att[...]
@@ -397,7 +389,7 @@
     result = (rows.astype(F32) + normed.astype(BF16).astype(F32)).astype(BF16)
     quad = out.shape[2]
     returns = [[copy(back.at[f, q], out.at[f, q], came(q)) for q in range(3)] for f in range(2)]
-    for q in range(3):
+    for q in (0, 2, 1):
         back[0, q] = result[q * quad:(q + 1) * quad]
         returns[0][q].start()
     out[0, 3] = result[3 * quad:]
@@ -415,13 +407,14 @@
     to_core.start()
     gatt[...] = dot_nn(grad_low, weight(3)).astype(BF16)
 
-    def backward(p):
-        @pl.loop(0, pairs)
-        def _(pair):
-            at = pl.ds(pl.multiple_of(pair * 6 * size, 128), 6 * size)
+    def backward(p, between):
+        for pair in range(pairs):
+            if pair == pairs // 2:
+                between()
+            at = slice(pair * 6 * size, (pair + 1) * 6 * size)
             piece = packed[p, :, at]
             g_at = p * per_piece * size + pair * 2 * size
-            g_pair = gatt[:, pl.ds(pl.multiple_of(g_at, 128), 2 * size)]
+            g_pair = gatt[:, g_at:g_at + 2 * size]
             outs = []
             for i in range(2):
                 head = p * per_piece + pair * 2 + i
@@ -441,26 +434,40 @@
                 outs += [g_q.astype(BF16), g_k.astype(BF16), g_val.astype(BF16)]
             gpacked[p, :, at] = jnp.concatenate(outs, axis=1)
 
-    backward(0)
-    to_core.wait_recv()
-    hsend[...] = (gsend[:, :, c].astype(F32) + grecv[...].astype(F32)).astype(BF16)
     to_x = copy(hsend.at[:, 1 - x], hrecv, x_dev)
-    to_x.start()
-    backward(1)
-    to_x.wait_recv()
-    zsend[...] = (hsend[:, x].astype(F32) + hrecv[...].astype(F32)).astype(BF16)
     to_z = [copy(zsend.at[zz], zrecv.at[k], zd) for k, (zz, zd) in enumerate(zip(zs, z_devs))]
-    for item in to_z:
-        item.start()
-    backward(2)
-    grad_rows = dot_nt(gpacked[0], weight(0))
-    grad_rows += dot_nt(gpacked[1], weight(1))
-    grad_rows += dot_nt(gpacked[2], weight(2))
-    grad_out = (grad_in + grad_rows.astype(BF16).astype(F32)).astype(BF16)
-    for q in range(3):
-        back[1, q] = grad_out[q * quad:(q + 1) * quad]
-        returns[1][q].start()
-    out[1, 3] = grad_out[3 * quad:]
+
+    def to_strips():
+        to_core.wait_recv()
+        hsend[...] = (gsend[:, :, c].astype(F32) + grecv[...].astype(F32)).astype(BF16)
+        to_x.start()
+
+    def to_levels():
+        to_x.wait_recv()
+        zsend[...] = (hsend[:, x].astype(F32) + hrecv[...].astype(F32)).astype(BF16)
+        for item in to_z:
+            item.start()
+
+    backward(0, to_strips)
+    backward(1, lambda: None)
+    backward(2, to_levels)
+
+    def grads_of(first, second):
+        total = 0.0
+        for p in range(3):
+            lhs = [gpacked[p, q * quad:(q + 1) * quad] for q in (first, second)]
+            total += dot_nt(jnp.concatenate(lhs, axis=0), weight(p))
+        for i, q in enumerate((first, second)):
+            added = total[i * quad:(i + 1) * quad].astype(BF16).astype(F32)
+            value = (grad_in[q * quad:(q + 1) * quad] + added).astype(BF16)
+            if q < 3:
+                back[1, q] = value
+                returns[1][q].start()
+            else:
+                out[1, q] = value
+
+    grads_of(0, 2)
+    grads_of(1, 3)
     total = zsend[z].astype(F32)
     for k, item in enumerate(to_z):
         item.wait_recv()
@@ -500,7 +507,7 @@
     own = jnp.concatenate(
         [qkv_weight.reshape(share, 3, chans).transpose(1, 0, 2), proj_weight.T[None]], axis=0
     )
-    copies = 6 + PIECES * (nz - 1) + 4 * PIECES + 6 + 2 + nz - 1
+    copies = 6 + PIECES * (2 * (nz - 1) + 2 * nz + 1) + 6 + 2 + nz - 1
     vmem = pl.BlockSpec(memory_space=pltpu.VMEM)
     scale_out = 1.0 / math.sqrt(count * space * lax.axis_size("dp"))
     out, pgrad = pl.pallas_call(

time: 78.7 us -> 77.6 us (0.986)
  Pallas kernels: 70.4 us -> 69.3 us
    pallas_call x1, Pallas kernels: 70.4 us -> 69.3 us  [fused_shards(): pl.pallas_call(functools.partial(slab_kernel, nz, heads, chans // heads,...]
where the time goes in v2:
time: 77.6 us; the launch traced here: 77.4 us
  Pallas kernels  69.3 us (89%)
  local copies, waits for them, and re-layouts  6.77 us (9%)
    pallas_call x1, Pallas kernels, fused_shards(): pl.pallas_call(functools.partial(slab_kernel, nz, heads, chans // heads,...  69.3 us
    unnamed x11, local copies, waits for them, and re-layouts  3 us
    squeeze x2, local copies, waits for them, and re-layouts, fused_shards(): return (grids[0], grids[1], pgrad.T)  1.68 us

profile of v2, /device:TPU:0, one launch (start us, length us, event | category | flops | bytes accessed | tf_op | source)
XLA Modules:
  0.0 77.4 jit_solution(10086803194697695234)
XLA Ops:
  0.6 0.0 copy-start.3
  0.6 0.8 fusion.2
  1.4 0.1 slice_add_fusion
  1.5 0.1 add_convert_fusion
  1.6 0.1 convert_element_type.22
  1.7 0.1 convert_element_type.24.region
  1.8 0.0 copy-done.3
  1.8 0.0 copy-start.4
  1.8 0.0 copy-start.1
  1.9 0.8 %copy-done.4 = bf16[768,48]{0,1:T(8,128)(2,1)S(1)} copy-done((bf16[768,48]{0,1:T(8,128)(2,1)S(1)}, bf16[768,48]{0,1:T(8,128)(2,1)}, u32[]{:S(2)}) %copy-start.4) | copy-done | bytes 73752
  2.7 0.1 copy-done.1
  2.8 0.0 copy-start.2
  2.8 0.1 stack.9
  2.9 0.9 %copy-done.2 = bf16[4,8,8,768]{3,2,1,0:T(8,128)(2,1)S(1)} copy-done((bf16[4,8,8,768]{3,2,1,0:T(8,128)(2,1)S(1)}, bf16[4,8,8,768]{3,2,1,0:T(8,128)(2,1)}, u32[]{:S(2)}) %copy-start.2) | copy-done | bytes 393240
  3.8 0.1 stack.10
  3.9 0.4 copy_bitcast_fusion
  4.3 0.0 copy-start
  4.3 0.2 reshape.42.fields
  4.5 0.5 copy-done
  5.0 69.3 %shard_map.85 = (bf16[2,4,64,768]{3,2,1,0:T(8,128)(2,1)S(1)}, f32[48,768]{1,0:T(8,128)S(1)}) custom-call(f32[12]{0:T(128)S(1)} %copy-done, bf16[2,4,64,768]{3,2,1,0:T(8,128)(2,1)S(1)} %reshape.42.fields, f32[1,256]{1,0:T(1,128)S(1)} %convert_element_type.24.region, bf16[4,48,768]{2,1,0:T(8,128)(2,1)S(1)} %pad_maximum_fusion.1.own), custom_call_target="tpu_custom_call" | custom-call | tf_op jit(solution)/shard_map/pallas_call | solution.py:513
  74.3 0.2 reshape.44
  74.4 0.3 fusion.1
  74.7 0.1 copy.19
  74.9 0.8 %squeeze.7 = bf16[4,8,8,768]{3,2,1,0:T(8,128)(2,1)} reshape(bf16[1,4,2,4,2,4,768]{6,5,4,3,2,1,0:T(4,128)(2,1)S(1)} %copy.19) | data formatting | bytes 786432 | tf_op jit(solution)/shard_map/squeeze | solution.py:545
  75.7 0.1 copy.18
  75.9 0.8 %squeeze.6 = bf16[4,8,8,768]{3,2,1,0:T(8,128)(2,1)} reshape(bf16[1,4,2,4,2,4,768]{6,5,4,3,2,1,0:T(4,128)(2,1)S(1)} %copy.18) | data formatting | bytes 786432 | tf_op jit(solution)/shard_map/squeeze | solution.py:545
  76.7 0.7 copy.28
  (4 shorter events, 0.1 us)
Async XLA Ops:
  0.6 1.2 %copy-start.3 = (bf16[48,2304]{1,0:T(8,128)(2,1)S(1)}, bf16[48,2304]{1,0:T(8,128)(2,1)}, u32[]{:S(2)}) copy-start(bf16[48,2304]{1,0:T(8,128)(2,1)} %param.9) | copy-start | bytes 663556
  1.8 0.9 %copy-start.4 = (bf16[768,48]{0,1:T(8,128)(2,1)S(1)}, bf16[768,48]{0,1:T(8,128)(2,1)}, u32[]{:S(2)}) copy-start(bf16[768,48]{0,1:T(8,128)(2,1)} %param.10) | copy-start | bytes 221188
  1.8 1.0 %copy-start.1 = (bf16[4,8,8,768]{3,2,1,0:T(8,128)(2,1)S(1)}, bf16[4,8,8,768]{3,2,1,0:T(8,128)(2,1)}, u32[]{:S(2)}) copy-start(bf16[4,8,8,768]{3,2,1,0:T(8,128)(2,1)} %param.6) | copy-start | bytes 1179652
  2.8 1.0 %copy-start.2 = (bf16[4,8,8,768]{3,2,1,0:T(8,128)(2,1)S(1)}, bf16[4,8,8,768]{3,2,1,0:T(8,128)(2,1)}, u32[]{:S(2)}) copy-start(bf16[4,8,8,768]{3,2,1,0:T(8,128)(2,1)} %param.7) | copy-start | bytes 1179652
  4.3 0.7 copy-start
